TPU v7x, 32 devices: a whole 2x2x4 slice. The times are simulated.
32 devices in a mesh: img: 8 (over y, x, core), view: 4 (over z).
Axes of the slice: x: 2, y: 2, z: 4, core: 2. Of those that a mesh axis runs over, the one named last changes fastest.
Arguments:
- images: float32 [2, 3072, 1024], P(None, ('img', 'view')), may hold values from -30 to 30, as said below
- views: float32 [2048, 1024], P('view'), may hold values from -5 to 5, as said below
Outputs:
- new_views: float32 [2048, 1024], P('view')
Inputs may be any that keep to these rules, and one draw needn't show every extreme that they name: `images`: real valued Fourier values. `views`: real valued Fourier values.
All inputs are finite; a program needn't handle non-finite values.
Results may differ from a plain program's by a relative error of at most 0.0003.
Values sent between devices are 32-bit elements; how exact they have to be, the bound alone decides.
A program may use at most 64 MiB of HBM per device.

v0:
```python
import math

import jax
import jax.numpy as jnp
from jax import lax
from jax.sharding import PartitionSpec as P

F = 1024


def on_device(images, views):
    gathered = lax.all_gather(images, "view", axis=1, tiled=True)
    beta = 1.6 / math.sqrt(F)
    current = views
    half_norm = 0.5 * jnp.sum(current * current, axis=1)
    scores = beta * (
        jnp.einsum("ibf,vf->ibv", gathered, current, precision=lax.Precision.HIGHEST) - half_norm
    )
    local_max = jnp.max(scores, axis=2)
    row_peak = lax.pmax(local_max, "view")
    row_total = lax.psum(jnp.sum(jnp.exp(scores - row_peak[:, :, None]), axis=2), "view")
    weights = jnp.exp(scores - row_peak[:, :, None]) / row_total[:, :, None]
    numerator = jnp.einsum("ibv,ibf->vf", weights, gathered, precision=lax.Precision.HIGHEST)
    weight_mass = jnp.sum(weights, axis=(0, 1))
    residual_sum = numerator - weight_mass[:, None] * current
    summed, total_mass = lax.psum((residual_sum, weight_mass), "img")
    current = current + summed / (total_mass[:, None] + 1.0)
    return current


def solution(mesh):
    placed = (P(None, ("img", "view"), None), P("view", None))
    return jax.shard_map(
        on_device, mesh=mesh, in_specs=placed, out_specs=P("view", None), check_vma=False
    )
```

profile of v0, /device:TPU:1, one launch (start us, length us, event | category | flops | bytes accessed | tf_op | source)
XLA Modules:
  0.0 183.2 jit_solution(16645716337715916240)
XLA Ops:
  6.5 0.0 copy-start
  6.5 0.0 all-gather.2.cloned.1.call-start
  6.5 0.7 all-gather.2.cloned.1.call-update
  7.3 0.0 all-reduce.2.cloned.1.call-start
  7.3 1.8 multiply_reduce_fusion
  9.1 65.4 %all-gather.2.cloned.1.call-done = f32[2,384,1024]{2,1,0:T(8,128)} async-done(((f32[2,96,1024]{2,1,0:T(8,128)}), f32[2,384,1024]{2,1,0:T(8,128)}) %all-gather.2.cloned.1.call-update) | async-done | bytes 3145744 | tf_op jit(solution)/shard_map/all_gather | solution.py:12
  74.5 0.0 copy-done
  74.5 7.8 %fusion.8 = (f32[2,384]{1,0:T(2,128)S(1)}, f32[2,384,512]{2,1,0:T(8,128)}) fusion(f32[512]{0:T(512)S(1)} %broadcast_multiply_fusion, f32[2,384,1024]{2,1,0:T(8,128)} %all-gather.2.cloned.1.call-done, f32[512,1024]{1,0:T(8,128)S(1)} %copy-done), kind=kOutput, calls=%fused_computation.12 | convolution fusion | flops 4833016832 | bytes 6820864 | tf_op jit(solution)/shard_map/ibf,vf->ibv/dot_general | solution.py:17
  82.3 7.3 %pmax.7 = f32[2,384]{1,0:T(2,128)S(1)} all-reduce(f32[2,384]{1,0:T(2,128)S(1)} %get-tuple-element.5), channel_id=1, replica_groups=mesh['img'=8,'view'=4] {'view'}, use_global_device_ids=true, to_apply=%region_2.0 | all-reduce | flops 768 | bytes 6144 | tf_op jit(solution)/shard_map/pmax | solution.py:20
  89.6 1.8 fusion.5
  91.4 7.4 %psum.21 = f32[2,384]{1,0:T(2,128)S(1)} all-reduce(f32[2,384]{1,0:T(2,128)S(1)} %fusion.5), channel_id=1, replica_groups=mesh['img'=8,'view'=4] {'view'}, use_global_device_ids=true, to_apply=%region_4.0 | all-reduce | flops 768 | bytes 6144 | tf_op jit(solution)/shard_map/psum | solution.py:21
  98.8 1.8 %fusion.6 = f32[512]{0:T(512)S(1)} fusion(f32[2,384]{1,0:T(2,128)S(1)} %psum.21, f32[2,384,512]{2,1,0:T(8,128)} %get-tuple-element.6, f32[2,384]{1,0:T(2,128)S(1)} %pmax.7), kind=kLoop, calls=%fused_computation.9 | loop fusion | flops 1179136 | bytes 1581056 | tf_op jit(solution)/shard_map/reduce_sum | solution.py:24
  100.7 8.9 %bitcast_subtract_fusion = f32[512,1024]{1,0:T(8,128)} fusion(f32[512,1024]{1,0:T(8,128)S(1)} %copy-done, f32[2,384,1024]{2,1,0:T(8,128)} %all-gather.2.cloned.1.call-done, f32[512]{0:T(512)S(1)} %fusion.6, f32[2,384,512]{2,1,0:T(8,128)} %get-tuple-element.6, f32[2,384]{1,0:T(2,128)S(1)} %psum.21, f32[2,384]{1,0:T(2,128)S(1)} %pmax.7), kind=kOutput, calls=%fused_computation | convolution fusion | flops 4833673216 | bytes 8921088 | tf_op jit(solution)/shard_map/ibv,ibf->vf/dot_general | solution.py:23
  109.6 0.0 all-reduce.2.cloned.1.call-update
  109.6 16.1 %psum.23 = f32[512]{0:T(512)S(1)} all-reduce(f32[512]{0:T(512)S(1)} %fusion.6), channel_id=1, replica_groups=mesh['img'=8,'view'=4] {'img'}, use_global_device_ids=true, to_apply=%region_7.0 | all-reduce | flops 512 | bytes 4096 | tf_op jit(solution)/shard_map/psum | solution.py:26
  125.7 47.2 %all-reduce.2.cloned.1.call-done = f32[512,1024]{1,0:T(8,128)} async-done(((f32[512,1024]{1,0:T(8,128)}), f32[512,1024]{1,0:T(8,128)}) %all-reduce.2.cloned.1.call-update) | async-done | bytes 2097168 | tf_op jit(solution)/shard_map/psum | solution.py:26
  172.9 3.5 %divide_add_fusion = f32[512,1024]{1,0:T(8,128)} fusion(f32[512,1024]{1,0:T(8,128)S(1)} %copy-done, f32[512,1024]{1,0:T(8,128)} %all-reduce.2.cloned.1.call-done, f32[512]{0:T(512)S(1)} %broadcast_add_fusion), kind=kLoop, calls=%fused_computation.3 | loop fusion | flops 1048576 | bytes 6293504 | tf_op jit(solution)/shard_map/add | solution.py:27
  (2 shorter events, 0.0 us)
Async XLA Ops:
  6.5 68.0 %copy-start = (f32[512,1024]{1,0:T(8,128)S(1)}, f32[512,1024]{1,0:T(8,128)}, u32[]{:S(2)}) copy-start(f32[512,1024]{1,0:T(8,128)} %param.3) | copy-start | bytes 6291460
  6.5 68.0 %all-gather.2.cloned.1.call-start = ((), (), s32[]{:S(2)}) async-start(), calls=%async_computation | async-start | bytes 3932160 | tf_op jit(solution)/shard_map/all_gather | solution.py:12
  7.3 165.7 %all-reduce.2.cloned.1.call-start = ((), (), s32[]{:S(2)}) async-start(), calls=%async_computation.1 | async-start | bytes 4194304 | tf_op jit(solution)/shard_map/psum | solution.py:26
Sparse Core Ops, SparseCore 0:
  8.9 65.5 all-gather.1
  109.7 63.1 all-reduce.1
where the time goes:
time: 185 us; the launch traced here: 183 us
  waiting for transfers between devices  113 us (61%)
  blocking collectives  30.8 us (17%)
  matrix products  16.7 us (9%)
  between operations  13.4 us (7%)
  other arithmetic  8.92 us (5%)
    all_gather x1, waiting for transfers between devices, on_device(): gathered = lax.all_gather(images, 'view', axis=1, tiled=True)  65.4 us
    psum x1, waiting for transfers between devices, on_device(): summed, total_mass = lax.psum((residual_sum, weight_mass), 'img')  47.2 us
    psum x1, blocking collectives, on_device(): summed, total_mass = lax.psum((residual_sum, weight_mass), 'img')  16.1 us
    dot_general x1, matrix products, on_device(): jnp.einsum('ibv,ibf->vf', weights, gathered, precision=lax.Precision.HIGH...  8.92 us
    dot_general x1, matrix products, on_device(): jnp.einsum('ibf,vf->ibv', gathered, current, precision=lax.Precision.HIGH...  7.8 us
    psum x1, blocking collectives, on_device(): lax.psum(jnp.sum(jnp.exp(scores - row_peak[:, :, None]), axis=2), 'view')  7.43 us
    pmax x1, blocking collectives, on_device(): row_peak = lax.pmax(local_max, 'view')  7.29 us
  transfers between devices with their start and end apart: 2, of which 2 were waited for; matrix products, arithmetic and copies ran while one was open for 1% of the time, Pallas kernels for 0%

commit v1 on v0

v1 whole, which is shorter than its diff:
```python
import functools
import math

import jax
import jax.numpy as jnp
from jax import lax
from jax.experimental import pallas as pl
from jax.experimental.pallas import tpu as pltpu
from jax.sharding import PartitionSpec as P

MESH = pl.DeviceIdType.MESH
F32 = jnp.float32
BF16 = jnp.bfloat16


def snake(c):
    row, col = c // 2, c % 2
    return 2 * row + col + (row % 2) * (1 - 2 * col)


def split(x):
    hi = x.astype(BF16)
    return hi, (x - hi.astype(F32)).astype(BF16)


def dot_nt(a, b):
    return lax.dot_general(a, b, (((1,), (1,)), ((), ())), preferred_element_type=F32)


def dot_nn(a, b):
    return lax.dot_general(a, b, (((1,), (0,)), ((), ())), preferred_element_type=F32)


class Ring:
    def __init__(self, chips, pos, core, z, buf, ring_send, ring_recv, sib_send, sib_recv):
        self.n, self.pos, self.core, self.z, self.buf = chips, pos, core, z, buf
        self.sems = ring_send, ring_recv, sib_send, sib_recv
        self.half = buf.shape[-1] // 2
        self.pending = []

    def chip(self, off):
        return snake(lax.rem(self.pos + off + self.n, self.n))

    def piece(self, off, core, h):
        return self.buf.at[self.chip(off) * 2 + core, :, pl.ds(h * self.half, self.half)]

    def hop(self, way, s, h, off):
        ref = self.piece(off, self.core, h)
        to = self.chip(1 if way == 0 else -1) * 2 + self.core
        return pltpu.make_async_remote_copy(
            ref, ref, self.sems[0].at[way, s - 1, h], self.sems[1].at[way, s - 1, h],
            device_id=(to, self.z), device_id_type=MESH)

    def cross(self, off, core, h):
        ref = self.piece(off, core, h)
        slot = off % self.n
        return pltpu.make_async_remote_copy(
            ref, ref, self.sems[2].at[slot, h], self.sems[3].at[slot, h],
            device_id=(self.chip(0) * 2 + 1 - self.core, self.z), device_id_type=MESH)

    def has(self, way, s, h):
        return s < self.n // 2 or (s == self.n // 2 and h == way)

    def go(self, copy):
        copy.start()
        self.pending.append(copy)

    def send_own(self, order):
        for h in order:
            for way in (0, 1):
                hh = h if way == 0 else order[1 - order.index(h)] if len(order) == 2 else h
                if self.has(way, 1, hh):
                    self.go(self.hop(way, 1, hh, 0))
        for h in order:
            self.go(self.cross(0, self.core, h))

    def arrive(self, way, s, h):
        off = -s if way == 0 else s
        self.hop(way, s, h, off).wait_recv()
        if self.has(way, s + 1, h):
            self.go(self.hop(way, s + 1, h, off))
        self.go(self.cross(off, self.core, h))

    def cross_wait(self, off, h):
        self.cross(off, 1 - self.core, h).wait_recv()

    def finish(self):
        for copy in self.pending:
            copy.wait_send()


def kernel(n_img, n_view, beta, images_ref, views_ref, out_ref,
           img, ihi, ilo, vws, vhi, vlo, hn, expo, phi, plo, stats, seen, num, rs_r, rs_l, rx_r, rx_l,
           mrow, mrx, res,
           in_sem, out_sem, ring_send, ring_recv, sib_send, sib_recv,
           oring_send, oring_recv, osib_send, osib_recv,
           v_send, v_recv, st_send, st_recv, r_send, r_recv, m_send, m_recv):
    i, z = lax.axis_index("img"), lax.axis_index("view")
    core, pos = lax.rem(i, 2), snake(i // 2)
    chips = n_img // 2
    rows = img.shape[1]
    part = vws.shape[1]
    feats = vws.shape[2]
    half = feats // 2

    own_img = pltpu.make_async_copy(images_ref, img.at[i], in_sem.at[0])
    own_vws = pltpu.make_async_copy(views_ref.at[pl.ds(i * part, part), :], vws.at[z], in_sem.at[1])
    own_img.start()
    own_vws.start()
    barrier = pltpu.get_barrier_semaphore()
    for d in range(1, n_img):
        pl.semaphore_signal(barrier, inc=1, device_id=(lax.rem(i + d, n_img), z), device_id_type=MESH)
    for d in range(1, n_view):
        pl.semaphore_signal(barrier, inc=1, device_id=(i, lax.rem(z + d, n_view)), device_id_type=MESH)
    own_img.wait()
    own_vws.wait()
    pl.semaphore_wait(barrier, n_img + n_view - 2)

    ring = Ring(chips, pos, core, z, img, ring_send, ring_recv, sib_send, sib_recv)
    ring.send_own((0, 1))

    def v_hop(way, j, block):
        ref = vws.at[block]
        to = z + 1 if way == 0 else z - 1
        return pltpu.make_async_remote_copy(
            ref, ref, v_send.at[way, j - 1], v_recv.at[way, j - 1], device_id=(i, to), device_id_type=MESH)

    def v_can(way):
        return z < n_view - 1 if way == 0 else z > 0

    for way in (0, 1):
        @pl.when(v_can(way))
        def _():
            v_hop(way, 1, z).start()

    def v_arrive(j):
        for way in (0, 1):
            block = z - j if way == 0 else z + j
            @pl.when(block >= 0 if way == 0 else block < n_view)
            def _():
                v_hop(way, j, block).wait_recv()

                @pl.when(v_can(way) if j < n_view - 1 else z < 0)
                def _():
                    v_hop(way, j + 1 if j < n_view - 1 else j, block).start()

    def prepare_views():
        current = vws[...].reshape(n_view * part, feats)
        hi, lo = split(current)
        vhi[...] = hi
        vlo[...] = lo
        hn[...] = jnp.broadcast_to(0.5 * jnp.sum(current * current, axis=1, keepdims=True), hn.shape)

    def score(off):
        c = ring.chip(off)
        x = img[pl.ds(2 * c, 2)].reshape(2 * rows, feats)
        hi, lo = split(x)
        ihi[c] = hi
        ilo[c] = lo
        s = dot_nt(vhi[...], hi) + dot_nt(vhi[...], lo) + dot_nt(vlo[...], hi)
        s = beta * (s - hn[:, 0:1])
        top = jnp.max(s, axis=0, keepdims=True)
        e = jnp.exp(s - top)
        expo[c] = e
        stats[c, 0:1, :] = top
        stats[c, 1:2, :] = jnp.sum(e, axis=0, keepdims=True)

    v_events = list(range(1, n_view))
    i_events = [(s, second) for s in range(1, chips // 2 + 1) for second in (0, 1)
                if s < chips // 2 or not second]
    order = []
    order += [("v", v) for v in v_events[:1]] + [("i", e) for e in i_events[:1]]
    order += [("v", v) for v in v_events[1:]] + [("i", e) for e in i_events[1:]]
    views_left = len(v_events)
    ready = [0]

    def flush():
        while ready:
            off = ready.pop(0)
            for h in (0, 1):
                ring.cross_wait(off, h)
            score(off)

    for kind, what in order:
        if kind == "v":
            v_arrive(what)
            views_left -= 1
            if views_left == 0:
                prepare_views()
                flush()
        else:
            s, second = what
            ring.arrive(0, s, second)
            ring.arrive(1, s, 1 - second)
            if s == chips // 2:
                ready += [s]
            elif second:
                ready += [-s, s]
            if views_left == 0:
                flush()

    sent = []
    for d in range(1, n_img):
        copy = pltpu.make_async_remote_copy(
            stats, seen.at[d - 1], st_send.at[d - 1], st_recv.at[d - 1],
            device_id=(lax.rem(i + d, n_img), z), device_id_type=MESH)
        copy.start()
        sent.append(copy)
    for copy in sent:
        copy.wait_recv()
    mass = jnp.zeros((n_view * part, 1), F32)
    for c in range(chips):
        mine = stats[c, 0:1, :]
        peak = mine
        for d in range(n_img - 1):
            peak = jnp.maximum(peak, seen[d, c, 0:1, :])
        factor = jnp.exp(mine - peak)
        total = stats[c, 1:2, :] * factor
        for d in range(n_img - 1):
            total = total + seen[d, c, 1:2, :] * jnp.exp(seen[d, c, 0:1, :] - peak)
        post = expo[c] * (factor / total)
        mass = mass + jnp.sum(post, axis=1, keepdims=True)
        hi, lo = split(post)
        phi[c] = hi
        plo[c] = lo

    eye = (lax.broadcasted_iota(jnp.int32, (part, 128), 0)
           == lax.broadcasted_iota(jnp.int32, (part, 128), 1))
    for b in range(n_view):
        col = mass[b * part:(b + 1) * part]
        row = jnp.sum(jnp.where(eye, col, 0.0), axis=0, keepdims=True)
        mrow[b] = jnp.broadcast_to(row, (8, 128))
    m_sent = []
    for d in range(1, n_view):
        to = lax.rem(z + d, n_view)
        copy = pltpu.make_async_remote_copy(
            mrow.at[to], mrx.at[d - 1], m_send.at[d - 1], m_recv.at[d - 1],
            device_id=(i, to), device_id_type=MESH)
        copy.start()
        m_sent.append(copy)

    def r_hop(way, b, h):
        src, dst = (rs_r, rx_r) if way == 0 else (rs_l, rx_l)
        to = z + 1 if way == 0 else z - 1
        return pltpu.make_async_remote_copy(
            src.at[h, b], dst.at[h, b], r_send.at[way, h, b], r_recv.at[way, h, b],
            device_id=(i, to), device_id_type=MESH)

    def from_start(way):
        return z == 0 if way == 0 else z == n_view - 1

    def passes(way, b):
        return z < b if way == 0 else z > b

    def blocks(way):
        return list(range(n_view - 1, 0, -1)) if way == 0 else list(range(n_view - 1))

    def numerators(h):
        total = jnp.zeros((n_view * part, half), F32)
        cols = pl.ds(h * half, half)
        for c in range(chips):
            total = total + (dot_nn(phi[c], ihi[c, :, cols]) + dot_nn(phi[c], ilo[c, :, cols])
                             + dot_nn(plo[c], ihi[c, :, cols]))
        num[h] = total.reshape(n_view, part, half)

    def reduce_start(h):
        for j in range(n_view - 1):
            for way in (0, 1):
                b = blocks(way)[j]

                @pl.when(from_start(way))
                def _():
                    src = rs_r if way == 0 else rs_l
                    src[h, b] = num[h, b]
                    r_hop(way, b, h).start()

    def reduce_pass(h):
        for j in range(n_view - 1):
            for way in (0, 1):
                b = blocks(way)[j]

                @pl.when(jnp.logical_and(jnp.logical_not(from_start(way)), passes(way, b)))
                def _():
                    src, got = (rs_r, rx_r) if way == 0 else (rs_l, rx_l)
                    r_hop(way, b, h).wait_recv()
                    src[h, b] = num[h, b] + got[h, b]
                    r_hop(way, b, h).start()

    out_ring = Ring(chips, pos, core, z, res, oring_send, oring_recv, osib_send, osib_recv)

    def last(h):
        for way in (0, 1):
            @pl.when(jnp.logical_not(from_start(way)))
            def _():
                got = rx_r if way == 0 else rx_l
                r_hop(way, z, h).wait_recv()
                num[h, z] = num[h, z] + got[h, z]

    def mass_total():
        for copy in m_sent:
            copy.wait_recv()
        row = mrow[z, 0:1, :]
        for d in range(n_view - 1):
            row = row + mrx[d, 0:1, :]
        return jnp.sum(jnp.where(eye, row, 0.0), axis=1, keepdims=True)

    for h in (0, 1):
        numerators(h)
        reduce_start(h)
    mass_all = None
    for h in (0, 1):
        reduce_pass(h)
        last(h)
        if h == 0:
            mass_all = mass_total()
        current = vws[z, :, pl.ds(h * half, half)]
        res[i, :, pl.ds(h * half, half)] = current + (num[h, z] - mass_all * current) / (mass_all + 1.0)
        out_ring.send_own((h,))

    stores = []

    def store(off, slot):
        c = out_ring.chip(off)
        copy = pltpu.make_async_copy(res.at[pl.ds(2 * c, 2)], out_ref.at[pl.ds(2 * c, 2)], out_sem.at[slot])
        copy.start()
        stores.append(copy)

    for s in range(1, chips // 2 + 1):
        for h in (0, 1):
            for way in (0, 1):
                if out_ring.has(way, s, h):
                    out_ring.arrive(way, s, h)
    for off in range(chips):
        for h in (0, 1):
            out_ring.cross_wait(off, h)
        store(off, off)

    ring.finish()
    out_ring.finish()
    for way in (0, 1):
        for j in range(1, n_view):
            block = z - (j - 1) if way == 0 else z + (j - 1)

            @pl.when(jnp.logical_and(v_can(way), block >= 0 if way == 0 else block < n_view))
            def _():
                v_hop(way, j, block).wait_send()
        for h in (0, 1):
            for b in blocks(way):
                @pl.when(passes(way, b))
                def _():
                    r_hop(way, b, h).wait_send()
    for copy in sent + m_sent:
        copy.wait_send()
    for copy in stores:
        copy.wait()


def on_device(n_img, n_view, images, views):
    inner, batch, feats = images.shape
    rows = inner * batch
    chips = n_img // 2
    part = views.shape[0] // n_img
    mine = n_view * part
    beta = 1.6 / math.sqrt(feats)
    half = feats // 2
    dma = pltpu.SemaphoreType.DMA
    vmem = pltpu.VMEM
    ring_sems = [dma((2, chips // 2, 2)), dma((2, chips // 2, 2)), dma((chips, 2)), dma((chips, 2))]
    out = pl.pallas_call(
        functools.partial(kernel, n_img, n_view, beta),
        out_shape=jax.ShapeDtypeStruct((n_img, part, feats), F32),
        in_specs=[pl.BlockSpec(memory_space=pl.ANY)] * 2,
        out_specs=pl.BlockSpec(memory_space=pl.ANY),
        scratch_shapes=[
            vmem((n_img, rows, feats), F32),
            vmem((chips, 2 * rows, feats), BF16),
            vmem((chips, 2 * rows, feats), BF16),
            vmem((n_view, part, feats), F32),
            vmem((mine, feats), BF16),
            vmem((mine, feats), BF16),
            vmem((mine, 128), F32),
            vmem((chips, mine, 2 * rows), F32),
            vmem((chips, mine, 2 * rows), BF16),
            vmem((chips, mine, 2 * rows), BF16),
            vmem((chips, 2, 2 * rows), F32),
            vmem((n_img - 1, chips, 2, 2 * rows), F32),
            vmem((2, n_view, part, half), F32),
            vmem((2, n_view, part, half), F32),
            vmem((2, n_view, part, half), F32),
            vmem((2, n_view, part, half), F32),
            vmem((2, n_view, part, half), F32),
            vmem((n_view, 8, 128), F32),
            vmem((n_view - 1, 8, 128), F32),
            vmem((n_img, part, feats), F32),
            dma((2,)), dma((chips,)),
        ] + ring_sems + ring_sems + [
            dma((2, n_view - 1)), dma((2, n_view - 1)),
            dma((n_img - 1,)), dma((n_img - 1,)),
            dma((2, 2, n_view)), dma((2, 2, n_view)),
            dma((n_view - 1,)), dma((n_view - 1,)),
        ],
        compiler_params=pltpu.CompilerParams(
            collective_id=0, has_side_effects=True, vmem_limit_bytes=48 * 1024 * 1024),
        cost_estimate=pl.CostEstimate(
            flops=12 * mine * n_img * rows * feats, bytes_accessed=16 * rows * feats, transcendentals=0),
    )(images.reshape(rows, feats), views)
    return out.reshape(n_img * part, feats)


def solution(mesh):
    placed = (P(None, ("img", "view"), None), P("view", None))
    return jax.shard_map(
        functools.partial(on_device, mesh.shape["img"], mesh.shape["view"]),
        mesh=mesh, in_specs=placed, out_specs=P("view", None), check_vma=False)
```

time: 185 us -> 83.1 us (0.45)
  waiting for transfers between devices: 113 us -> 0 us
  Pallas kernels: 0 us -> 78.9 us
  blocking collectives: 30.8 us -> 0 us
  matrix products: 16.7 us -> 0 us
  between operations: 13.4 us -> 0.01 us
  other arithmetic: 8.92 us -> 0 us
  local copies, waits for them, and re-layouts: 0.01 us -> 4.04 us
    pallas_call x0 -> x1, Pallas kernels: none -> 78.9 us  [on_device(): pl.pallas_call(functools.partial(kernel, n_img, n_view, beta), out_shape=...]
    all_gather x1 -> x0, waiting for transfers between devices: 65.4 us -> none  [on_device(): gathered = lax.all_gather(images, 'view', axis=1, tiled=True)]
    psum x1 -> x0, waiting for transfers between devices: 47.2 us -> none  [on_device(): summed, total_mass = lax.psum((residual_sum, weight_mass), 'img')]
    psum x2 -> x0, blocking collectives: 23.5 us -> none  [the longest x1 16.1 us: on_device(): summed, total_mass = lax.psum((residual_sum, weight_mass), 'img')]
    dot_general x2 -> x0, matrix products: 16.7 us -> none  [the longest x1 8.92 us: on_device(): jnp.einsum('ibv,ibf->vf', weights, gathered, precision=lax.Precision.HIGH...]
    pmax x1 -> x0, blocking collectives: 7.29 us -> none  [on_device(): row_peak = lax.pmax(local_max, 'view')]
    reduce_sum x3 -> x0, other arithmetic: 5.45 us -> none  [the longest x1 1.85 us: on_device(): weight_mass = jnp.sum(weights, axis=(0, 1))]
    unnamed x2 -> x5, local copies, waits for them, and re-layouts: 0.01 us -> 4.04 us
  transfers between devices with their start and end apart: 2 -> 0, of which waited for: 2 -> 0; matrix products, arithmetic and copies ran while one was open for 1% -> 0% of each run, Pallas kernels for 0% -> 0%
where the time goes in v1:
time: 83.1 us; the launch traced here: 82.9 us
  Pallas kernels  78.9 us (95%)
  local copies, waits for them, and re-layouts  4.04 us (5%)
    pallas_call x1, Pallas kernels, on_device(): pl.pallas_call(functools.partial(kernel, n_img, n_view, beta), out_shape=...  78.9 us
    unnamed x5, local copies, waits for them, and re-layouts  4.04 us

profile of v1, /device:TPU:1, one launch (start us, length us, event | category | flops | bytes accessed | tf_op | source)
XLA Modules:
  0.0 82.9 jit_solution(15634836339919038750)
XLA Ops:
  0.0 0.0 copy-start
  0.0 1.6 %copy-done = f32[512,1024]{1,0:T(8,128)S(1)} copy-done((f32[512,1024]{1,0:T(8,128)S(1)}, f32[512,1024]{1,0:T(8,128)}, u32[]{:S(2)}) %copy-start) | copy-done | bytes 2097176
  1.6 0.0 copy-start.1
  1.6 1.1 %copy-done.1 = f32[2,96,1024]{2,1,0:T(8,128)S(1)} copy-done((f32[2,96,1024]{2,1,0:T(8,128)S(1)}, f32[2,96,1024]{2,1,0:T(8,128)}, u32[]{:S(2)}) %copy-start.1) | copy-done | bytes 786456
  2.7 78.9 %shard_map.28 = f32[8,64,1024]{2,1,0:T(8,128)S(1)} custom-call(f32[192,1024]{1,0:T(8,128)S(1)} %bitcast.3, f32[512,1024]{1,0:T(8,128)S(1)} %copy-done), custom_call_target="tpu_custom_call" | custom-call | flops 4831838208 | bytes 3145728 | tf_op jit(solution)/shard_map/pallas_call | solution.py:369
  81.6 1.3 %copy.4 = f32[512,1024]{1,0:T(8,128)} copy(f32[512,1024]{1,0:T(8,128)S(1)} %bitcast.2) | data formatting | bytes 4194304
Async XLA Ops:
  0.0 1.6 %copy-start = (f32[512,1024]{1,0:T(8,128)S(1)}, f32[512,1024]{1,0:T(8,128)}, u32[]{:S(2)}) copy-start(f32[512,1024]{1,0:T(8,128)} %views_ref.1) | copy-start | bytes 6291460
  1.6 1.1 %copy-start.1 = (f32[2,96,1024]{2,1,0:T(8,128)S(1)}, f32[2,96,1024]{2,1,0:T(8,128)}, u32[]{:S(2)}) copy-start(f32[2,96,1024]{2,1,0:T(8,128)} %param.2) | copy-start | bytes 2359300

commit v2 on v1

--- a/solution.py
+++ b/solution.py
@@ -81,6 +81,12 @@
             self.go(self.hop(way, s + 1, h, off))
         self.go(self.cross(off, self.core, h))
 
+    def direct(self, off, h, mine):
+        ref = self.piece(0 if mine else -off, self.core, h)
+        return pltpu.make_async_remote_copy(
+            ref, ref, self.sems[0].at[off - 1, h], self.sems[1].at[off - 1, h],
+            device_id=(self.chip(off) * 2 + self.core, self.z), device_id_type=MESH)
+
     def cross_wait(self, off, h):
         self.cross(off, 1 - self.core, h).wait_recv()
 
@@ -90,7 +96,7 @@
 
 
 def kernel(n_img, n_view, beta, images_ref, views_ref, out_ref,
-           img, ihi, ilo, vws, vhi, vlo, hn, expo, phi, plo, stats, seen, num, rs_r, rs_l, rx_r, rx_l,
+           img, ihi, ilo, vws, vhi, vlo, hn, expo, phi, plo, stats, seen, num, rx,
            mrow, mrx, res,
            in_sem, out_sem, ring_send, ring_recv, sib_send, sib_recv,
            oring_send, oring_recv, osib_send, osib_recv,
@@ -169,8 +175,8 @@
     i_events = [(s, second) for s in range(1, chips // 2 + 1) for second in (0, 1)
                 if s < chips // 2 or not second]
     order = []
-    order += [("v", v) for v in v_events[:1]] + [("i", e) for e in i_events[:1]]
-    order += [("v", v) for v in v_events[1:]] + [("i", e) for e in i_events[1:]]
+    order += [("v", v) for v in v_events[:2]] + [("i", e) for e in i_events[:1]]
+    order += [("v", v) for v in v_events[2:]] + [("i", e) for e in i_events[1:]]
     views_left = len(v_events)
     ready = [0]
 
@@ -239,21 +245,7 @@
         copy.start()
         m_sent.append(copy)
 
-    def r_hop(way, b, h):
-        src, dst = (rs_r, rx_r) if way == 0 else (rs_l, rx_l)
-        to = z + 1 if way == 0 else z - 1
-        return pltpu.make_async_remote_copy(
-            src.at[h, b], dst.at[h, b], r_send.at[way, h, b], r_recv.at[way, h, b],
-            device_id=(i, to), device_id_type=MESH)
-
-    def from_start(way):
-        return z == 0 if way == 0 else z == n_view - 1
-
-    def passes(way, b):
-        return z < b if way == 0 else z > b
-
-    def blocks(way):
-        return list(range(n_view - 1, 0, -1)) if way == 0 else list(range(n_view - 1))
+    r_sent = []
 
     def numerators(h):
         total = jnp.zeros((n_view * part, half), F32)
@@ -262,39 +254,22 @@
             total = total + (dot_nn(phi[c], ihi[c, :, cols]) + dot_nn(phi[c], ilo[c, :, cols])
                              + dot_nn(plo[c], ihi[c, :, cols]))
         num[h] = total.reshape(n_view, part, half)
-
-    def reduce_start(h):
-        for j in range(n_view - 1):
-            for way in (0, 1):
-                b = blocks(way)[j]
-
-                @pl.when(from_start(way))
-                def _():
-                    src = rs_r if way == 0 else rs_l
-                    src[h, b] = num[h, b]
-                    r_hop(way, b, h).start()
-
-    def reduce_pass(h):
-        for j in range(n_view - 1):
-            for way in (0, 1):
-                b = blocks(way)[j]
-
-                @pl.when(jnp.logical_and(jnp.logical_not(from_start(way)), passes(way, b)))
-                def _():
-                    src, got = (rs_r, rx_r) if way == 0 else (rs_l, rx_l)
-                    r_hop(way, b, h).wait_recv()
-                    src[h, b] = num[h, b] + got[h, b]
-                    r_hop(way, b, h).start()
+        for d in range(1, n_view):
+            to = lax.rem(z + d, n_view)
+            copy = pltpu.make_async_remote_copy(
+                num.at[h, to], rx.at[h, d - 1], r_send.at[h, d - 1], r_recv.at[h, d - 1],
+                device_id=(i, to), device_id_type=MESH)
+            copy.start()
+            r_sent.append(copy)
 
     out_ring = Ring(chips, pos, core, z, res, oring_send, oring_recv, osib_send, osib_recv)
 
-    def last(h):
-        for way in (0, 1):
-            @pl.when(jnp.logical_not(from_start(way)))
-            def _():
-                got = rx_r if way == 0 else rx_l
-                r_hop(way, z, h).wait_recv()
-                num[h, z] = num[h, z] + got[h, z]
+    def summed(h):
+        total = num[h, z]
+        for d in range(n_view - 1):
+            r_sent[h * (n_view - 1) + d].wait_recv()
+            total = total + rx[h, d]
+        return total
 
     def mass_total():
         for copy in m_sent:
@@ -306,34 +281,27 @@
 
     for h in (0, 1):
         numerators(h)
-        reduce_start(h)
-    mass_all = None
+    mass_all = mass_total()
     for h in (0, 1):
-        reduce_pass(h)
-        last(h)
-        if h == 0:
-            mass_all = mass_total()
         current = vws[z, :, pl.ds(h * half, half)]
-        res[i, :, pl.ds(h * half, half)] = current + (num[h, z] - mass_all * current) / (mass_all + 1.0)
-        out_ring.send_own((h,))
+        res[i, :, pl.ds(h * half, half)] = current + (summed(h) - mass_all * current) / (mass_all + 1.0)
+        for off in range(1, chips):
+            out_ring.go(out_ring.direct(off, h, True))
+        out_ring.go(out_ring.cross(0, core, h))
+
+    for h in (0, 1):
+        for off in range(1, chips):
+            out_ring.direct(off, h, False).wait_recv()
+            out_ring.go(out_ring.cross(-off, core, h))
 
     stores = []
-
-    def store(off, slot):
-        c = out_ring.chip(off)
-        copy = pltpu.make_async_copy(res.at[pl.ds(2 * c, 2)], out_ref.at[pl.ds(2 * c, 2)], out_sem.at[slot])
+    for off in range(chips):
+        for h in (0, 1):
+            out_ring.cross_wait(-off, h)
+        c = out_ring.chip(-off)
+        copy = pltpu.make_async_copy(res.at[pl.ds(2 * c, 2)], out_ref.at[pl.ds(2 * c, 2)], out_sem.at[off])
         copy.start()
         stores.append(copy)
-
-    for s in range(1, chips // 2 + 1):
-        for h in (0, 1):
-            for way in (0, 1):
-                if out_ring.has(way, s, h):
-                    out_ring.arrive(way, s, h)
-    for off in range(chips):
-        for h in (0, 1):
-            out_ring.cross_wait(off, h)
-        store(off, off)
 
     ring.finish()
     out_ring.finish()
@@ -344,12 +312,7 @@
             @pl.when(jnp.logical_and(v_can(way), block >= 0 if way == 0 else block < n_view))
             def _():
                 v_hop(way, j, block).wait_send()
-        for h in (0, 1):
-            for b in blocks(way):
-                @pl.when(passes(way, b))
-                def _():
-                    r_hop(way, b, h).wait_send()
-    for copy in sent + m_sent:
+    for copy in sent + m_sent + r_sent:
         copy.wait_send()
     for copy in stores:
         copy.wait()
@@ -369,7 +332,7 @@
     out = pl.pallas_call(
         functools.partial(kernel, n_img, n_view, beta),
         out_shape=jax.ShapeDtypeStruct((n_img, part, feats), F32),
-        in_specs=[pl.BlockSpec(memory_space=pl.ANY)] * 2,
+        in_specs=[pl.BlockSpec(memory_space=pltpu.HBM)] * 2,
         out_specs=pl.BlockSpec(memory_space=pl.ANY),
         scratch_shapes=[
             vmem((n_img, rows, feats), F32),
@@ -385,18 +348,15 @@
             vmem((chips, 2, 2 * rows), F32),
             vmem((n_img - 1, chips, 2, 2 * rows), F32),
             vmem((2, n_view, part, half), F32),
-            vmem((2, n_view, part, half), F32),
-            vmem((2, n_view, part, half), F32),
-            vmem((2, n_view, part, half), F32),
-            vmem((2, n_view, part, half), F32),
+            vmem((2, n_view - 1, part, half), F32),
             vmem((n_view, 8, 128), F32),
             vmem((n_view - 1, 8, 128), F32),
             vmem((n_img, part, feats), F32),
             dma((2,)), dma((chips,)),
-        ] + ring_sems + ring_sems + [
+        ] + ring_sems + [dma((chips - 1, 2)), dma((chips - 1, 2)), dma((chips, 2)), dma((chips, 2))] + [
             dma((2, n_view - 1)), dma((2, n_view - 1)),
             dma((n_img - 1,)), dma((n_img - 1,)),
-            dma((2, 2, n_view)), dma((2, 2, n_view)),
+            dma((2, n_view - 1)), dma((2, n_view - 1)),
             dma((n_view - 1,)), dma((n_view - 1,)),
         ],
         compiler_params=pltpu.CompilerParams(

time: 83.1 us -> 77.6 us (0.934); the launches traced: 82.9 us -> 76.5 us
  Pallas kernels: 78.9 us -> 72.4 us
    pallas_call x1, Pallas kernels: 78.9 us -> 72.4 us  [on_device(): pl.pallas_call(functools.partial(kernel, n_img, n_view, beta), out_shape=...]
where the time goes in v2:
time: 77.6 us; the launch traced here: 76.5 us
  Pallas kernels  72.4 us (93%)
  local copies, waits for them, and re-layouts  4.04 us (5%)
    pallas_call x1, Pallas kernels, on_device(): pl.pallas_call(functools.partial(kernel, n_img, n_view, beta), out_shape=...  72.4 us
    unnamed x5, local copies, waits for them, and re-layouts  4.04 us

profile of v2, /device:TPU:1, one launch (start us, length us, event | category | flops | bytes accessed | tf_op | source)
XLA Modules:
  0.0 76.5 jit_solution(11181686931189814560)
XLA Ops:
  0.0 0.0 copy-start
  0.0 1.6 %copy-done = f32[512,1024]{1,0:T(8,128)S(1)} copy-done((f32[512,1024]{1,0:T(8,128)S(1)}, f32[512,1024]{1,0:T(8,128)}, u32[]{:S(2)}) %copy-start) | copy-done | bytes 2097176
  1.6 0.0 copy-start.1
  1.6 1.1 %copy-done.1 = f32[2,96,1024]{2,1,0:T(8,128)S(1)} copy-done((f32[2,96,1024]{2,1,0:T(8,128)S(1)}, f32[2,96,1024]{2,1,0:T(8,128)}, u32[]{:S(2)}) %copy-start.1) | copy-done | bytes 786456
  2.7 72.4 %shard_map.28 = f32[8,64,1024]{2,1,0:T(8,128)S(1)} custom-call(f32[192,1024]{1,0:T(8,128)S(1)} %bitcast.3, f32[512,1024]{1,0:T(8,128)S(1)} %copy-done), custom_call_target="tpu_custom_call" | custom-call | flops 4831838208 | bytes 3145728 | tf_op jit(solution)/shard_map/pallas_call | solution.py:332
  75.2 1.3 %copy.4 = f32[512,1024]{1,0:T(8,128)} copy(f32[512,1024]{1,0:T(8,128)S(1)} %bitcast.2) | data formatting | bytes 4194304
Async XLA Ops:
  0.0 1.6 %copy-start = (f32[512,1024]{1,0:T(8,128)S(1)}, f32[512,1024]{1,0:T(8,128)}, u32[]{:S(2)}) copy-start(f32[512,1024]{1,0:T(8,128)} %views_ref.1) | copy-start | bytes 6291460
  1.6 1.1 %copy-start.1 = (f32[2,96,1024]{2,1,0:T(8,128)S(1)}, f32[2,96,1024]{2,1,0:T(8,128)}, u32[]{:S(2)}) copy-start(f32[2,96,1024]{2,1,0:T(8,128)} %param.2) | copy-start | bytes 2359300

commit v3 on v2

--- a/solution.py
+++ b/solution.py
@@ -125,45 +125,55 @@
     ring = Ring(chips, pos, core, z, img, ring_send, ring_recv, sib_send, sib_recv)
     ring.send_own((0, 1))
 
-    def v_hop(way, j, block):
-        ref = vws.at[block]
+    def v_hop(way, j, block, h):
+        ref = vws.at[block, :, pl.ds(h * half, half)]
         to = z + 1 if way == 0 else z - 1
         return pltpu.make_async_remote_copy(
-            ref, ref, v_send.at[way, j - 1], v_recv.at[way, j - 1], device_id=(i, to), device_id_type=MESH)
+            ref, ref, v_send.at[way, j - 1, h], v_recv.at[way, j - 1, h], device_id=(i, to), device_id_type=MESH)
 
     def v_can(way):
         return z < n_view - 1 if way == 0 else z > 0
 
-    for way in (0, 1):
-        @pl.when(v_can(way))
-        def _():
-            v_hop(way, 1, z).start()
-
-    def v_arrive(j):
+    for h in (0, 1):
+        for way in (0, 1):
+            @pl.when(v_can(way))
+            def _():
+                v_hop(way, 1, z, h).start()
+
+    def prepare_block(block):
+        current = vws[block]
+        hi, lo = split(current)
+        at = pl.ds(pl.multiple_of(block * part, part), part)
+        vhi[at, :] = hi
+        vlo[at, :] = lo
+        hn[at, :] = jnp.broadcast_to(0.5 * jnp.sum(current * current, axis=1, keepdims=True), (part, 128))
+
+    def v_arrive(j, h):
         for way in (0, 1):
             block = z - j if way == 0 else z + j
             @pl.when(block >= 0 if way == 0 else block < n_view)
             def _():
-                v_hop(way, j, block).wait_recv()
-
-                @pl.when(v_can(way) if j < n_view - 1 else z < 0)
-                def _():
-                    v_hop(way, j + 1 if j < n_view - 1 else j, block).start()
-
-    def prepare_views():
-        current = vws[...].reshape(n_view * part, feats)
-        hi, lo = split(current)
-        vhi[...] = hi
-        vlo[...] = lo
-        hn[...] = jnp.broadcast_to(0.5 * jnp.sum(current * current, axis=1, keepdims=True), hn.shape)
+                v_hop(way, j, block, h).wait_recv()
+                if j < n_view - 1:
+                    @pl.when(v_can(way))
+                    def _():
+                        v_hop(way, j + 1, block, h).start()
+                if h == 1:
+                    prepare_block(block)
+
+    def prepare_images(off):
+        c = ring.chip(off)
+        for h in (0, 1):
+            ring.cross_wait(off, h)
+        hi, lo = split(img[pl.ds(2 * c, 2)].reshape(2 * rows, feats))
+        ihi[c] = hi
+        ilo[c] = lo
+
+    prepare_block(z)
 
     def score(off):
         c = ring.chip(off)
-        x = img[pl.ds(2 * c, 2)].reshape(2 * rows, feats)
-        hi, lo = split(x)
-        ihi[c] = hi
-        ilo[c] = lo
-        s = dot_nt(vhi[...], hi) + dot_nt(vhi[...], lo) + dot_nt(vlo[...], hi)
+        s = dot_nt(vhi[...], ihi[c]) + dot_nt(vhi[...], ilo[c]) + dot_nt(vlo[...], ihi[c])
         s = beta * (s - hn[:, 0:1])
         top = jnp.max(s, axis=0, keepdims=True)
         e = jnp.exp(s - top)
@@ -171,28 +181,29 @@
         stats[c, 0:1, :] = top
         stats[c, 1:2, :] = jnp.sum(e, axis=0, keepdims=True)
 
-    v_events = list(range(1, n_view))
+    v_events = [(j, h) for j in range(1, n_view) for h in (0, 1)]
     i_events = [(s, second) for s in range(1, chips // 2 + 1) for second in (0, 1)
                 if s < chips // 2 or not second]
     order = []
-    order += [("v", v) for v in v_events[:2]] + [("i", e) for e in i_events[:1]]
-    order += [("v", v) for v in v_events[2:]] + [("i", e) for e in i_events[1:]]
+    order += [("v", v) for v in v_events[:4]] + [("i", e) for e in i_events[:1]]
+    order += [("v", v) for v in v_events[4:]] + [("i", e) for e in i_events[1:]]
     views_left = len(v_events)
     ready = [0]
 
     def flush():
         while ready:
             off = ready.pop(0)
-            for h in (0, 1):
-                ring.cross_wait(off, h)
+            if off:
+                prepare_images(off)
             score(off)
 
     for kind, what in order:
         if kind == "v":
-            v_arrive(what)
+            v_arrive(*what)
+            if views_left == len(v_events):
+                prepare_images(0)
             views_left -= 1
             if views_left == 0:
-                prepare_views()
                 flush()
         else:
             s, second = what
@@ -311,7 +322,8 @@
 
             @pl.when(jnp.logical_and(v_can(way), block >= 0 if way == 0 else block < n_view))
             def _():
-                v_hop(way, j, block).wait_send()
+                for h in (0, 1):
+                    v_hop(way, j, block, h).wait_send()
     for copy in sent + m_sent + r_sent:
         copy.wait_send()
     for copy in stores:
@@ -332,7 +344,7 @@
     out = pl.pallas_call(
         functools.partial(kernel, n_img, n_view, beta),
         out_shape=jax.ShapeDtypeStruct((n_img, part, feats), F32),
-        in_specs=[pl.BlockSpec(memory_space=pltpu.HBM)] * 2,
+        in_specs=[pl.BlockSpec(memory_space=pl.ANY)] * 2,
         out_specs=pl.BlockSpec(memory_space=pl.ANY),
         scratch_shapes=[
             vmem((n_img, rows, feats), F32),
@@ -354,13 +366,13 @@
             vmem((n_img, part, feats), F32),
             dma((2,)), dma((chips,)),
         ] + ring_sems + [dma((chips - 1, 2)), dma((chips - 1, 2)), dma((chips, 2)), dma((chips, 2))] + [
-            dma((2, n_view - 1)), dma((2, n_view - 1)),
+            dma((2, n_view - 1, 2)), dma((2, n_view - 1, 2)),
             dma((n_img - 1,)), dma((n_img - 1,)),
             dma((2, n_view - 1)), dma((2, n_view - 1)),
             dma((n_view - 1,)), dma((n_view - 1,)),
         ],
         compiler_params=pltpu.CompilerParams(
-            collective_id=0, has_side_effects=True, vmem_limit_bytes=48 * 1024 * 1024),
+            collective_id=0, has_side_effects=True, vmem_limit_bytes=51 * 1024 * 1024),
         cost_estimate=pl.CostEstimate(
             flops=12 * mine * n_img * rows * feats, bytes_accessed=16 * rows * feats, transcendentals=0),
     )(images.reshape(rows, feats), views)

time: 77.6 us -> 76.1 us (0.981)
  local copies, waits for them, and re-layouts: 4.04 us -> 2.45 us
    unnamed x5 -> x3, local copies, waits for them, and re-layouts: 4.04 us -> 2.45 us
where the time goes in v3:
time: 76.1 us; the launch traced here: 74.9 us
  Pallas kernels  72.5 us (95%)
  local copies, waits for them, and re-layouts  2.45 us (3%)
    pallas_call x1, Pallas kernels, on_device(): pl.pallas_call(functools.partial(kernel, n_img, n_view, beta), out_shape=...  72.5 us
    unnamed x3, local copies, waits for them, and re-layouts  2.45 us

profile of v3, /device:TPU:1, one launch (start us, length us, event | category | flops | bytes accessed | tf_op | source)
XLA Modules:
  0.0 74.9 jit_solution(11917003716519816610)
XLA Ops:
  0.0 0.0 copy-start
  0.0 1.1 %copy-done = f32[2,96,1024]{2,1,0:T(8,128)S(1)} copy-done((f32[2,96,1024]{2,1,0:T(8,128)S(1)}, f32[2,96,1024]{2,1,0:T(8,128)}, u32[]{:S(2)}) %copy-start) | copy-done | bytes 786456
  1.1 72.5 %shard_map.28 = f32[8,64,1024]{2,1,0:T(8,128)S(1)} custom-call(f32[192,1024]{1,0:T(8,128)S(1)} %bitcast.3, f32[512,1024]{1,0:T(8,128)} %views_ref.1), custom_call_target="tpu_custom_call" | custom-call | flops 4831838208 | bytes 3145728 | tf_op jit(solution)/shard_map/pallas_call | solution.py:344
  73.6 1.3 %copy.4 = f32[512,1024]{1,0:T(8,128)} copy(f32[512,1024]{1,0:T(8,128)S(1)} %bitcast.2) | data formatting | bytes 4194304
Async XLA Ops:
  0.0 1.1 %copy-start = (f32[2,96,1024]{2,1,0:T(8,128)S(1)}, f32[2,96,1024]{2,1,0:T(8,128)}, u32[]{:S(2)}) copy-start(f32[2,96,1024]{2,1,0:T(8,128)} %param.2) | copy-start | bytes 2359300

commit v4 on v3

--- a/solution.py
+++ b/solution.py
@@ -11,6 +11,7 @@
 MESH = pl.DeviceIdType.MESH
 F32 = jnp.float32
 BF16 = jnp.bfloat16
+PIECES = 4
 
 
 def snake(c):
@@ -32,10 +33,10 @@
 
 
 class Ring:
-    def __init__(self, chips, pos, core, z, buf, ring_send, ring_recv, sib_send, sib_recv):
+    def __init__(self, chips, pos, core, z, buf, parts, ring_send, ring_recv, sib_send, sib_recv):
         self.n, self.pos, self.core, self.z, self.buf = chips, pos, core, z, buf
         self.sems = ring_send, ring_recv, sib_send, sib_recv
-        self.half = buf.shape[-1] // 2
+        self.half = buf.shape[-1] // parts
         self.pending = []
 
     def chip(self, off):
@@ -108,6 +109,7 @@
     part = vws.shape[1]
     feats = vws.shape[2]
     half = feats // 2
+    width = feats // PIECES
 
     own_img = pltpu.make_async_copy(images_ref, img.at[i], in_sem.at[0])
     own_vws = pltpu.make_async_copy(views_ref.at[pl.ds(i * part, part), :], vws.at[z], in_sem.at[1])
@@ -122,7 +124,7 @@
     own_vws.wait()
     pl.semaphore_wait(barrier, n_img + n_view - 2)
 
-    ring = Ring(chips, pos, core, z, img, ring_send, ring_recv, sib_send, sib_recv)
+    ring = Ring(chips, pos, core, z, img, 2, ring_send, ring_recv, sib_send, sib_recv)
     ring.send_own((0, 1))
 
     def v_hop(way, j, block, h):
@@ -259,12 +261,12 @@
     r_sent = []
 
     def numerators(h):
-        total = jnp.zeros((n_view * part, half), F32)
-        cols = pl.ds(h * half, half)
+        total = jnp.zeros((n_view * part, width), F32)
+        cols = pl.ds(h * width, width)
         for c in range(chips):
             total = total + (dot_nn(phi[c], ihi[c, :, cols]) + dot_nn(phi[c], ilo[c, :, cols])
                              + dot_nn(plo[c], ihi[c, :, cols]))
-        num[h] = total.reshape(n_view, part, half)
+        num[h] = total.reshape(n_view, part, width)
         for d in range(1, n_view):
             to = lax.rem(z + d, n_view)
             copy = pltpu.make_async_remote_copy(
@@ -273,7 +275,7 @@
             copy.start()
             r_sent.append(copy)
 
-    out_ring = Ring(chips, pos, core, z, res, oring_send, oring_recv, osib_send, osib_recv)
+    out_ring = Ring(chips, pos, core, z, res, PIECES, oring_send, oring_recv, osib_send, osib_recv)
 
     def summed(h):
         total = num[h, z]
@@ -290,24 +292,27 @@
             row = row + mrx[d, 0:1, :]
         return jnp.sum(jnp.where(eye, row, 0.0), axis=1, keepdims=True)
 
-    for h in (0, 1):
+    def gather(h):
+        for off in range(1, chips):
+            out_ring.direct(off, h, False).wait_recv()
+            out_ring.go(out_ring.cross(-off, core, h))
+
+    for h in range(PIECES):
         numerators(h)
     mass_all = mass_total()
-    for h in (0, 1):
-        current = vws[z, :, pl.ds(h * half, half)]
-        res[i, :, pl.ds(h * half, half)] = current + (summed(h) - mass_all * current) / (mass_all + 1.0)
+    for h in range(PIECES):
+        current = vws[z, :, pl.ds(h * width, width)]
+        res[i, :, pl.ds(h * width, width)] = current + (summed(h) - mass_all * current) / (mass_all + 1.0)
         for off in range(1, chips):
             out_ring.go(out_ring.direct(off, h, True))
         out_ring.go(out_ring.cross(0, core, h))
-
-    for h in (0, 1):
-        for off in range(1, chips):
-            out_ring.direct(off, h, False).wait_recv()
-            out_ring.go(out_ring.cross(-off, core, h))
+        if h > 0:
+            gather(h - 1)
+    gather(PIECES - 1)
 
     stores = []
     for off in range(chips):
-        for h in (0, 1):
+        for h in range(PIECES):
             out_ring.cross_wait(-off, h)
         c = out_ring.chip(-off)
         copy = pltpu.make_async_copy(res.at[pl.ds(2 * c, 2)], out_ref.at[pl.ds(2 * c, 2)], out_sem.at[off])
@@ -337,7 +342,7 @@
     part = views.shape[0] // n_img
     mine = n_view * part
     beta = 1.6 / math.sqrt(feats)
-    half = feats // 2
+    width = feats // PIECES
     dma = pltpu.SemaphoreType.DMA
     vmem = pltpu.VMEM
     ring_sems = [dma((2, chips // 2, 2)), dma((2, chips // 2, 2)), dma((chips, 2)), dma((chips, 2))]
@@ -359,16 +364,17 @@
             vmem((chips, mine, 2 * rows), BF16),
             vmem((chips, 2, 2 * rows), F32),
             vmem((n_img - 1, chips, 2, 2 * rows), F32),
-            vmem((2, n_view, part, half), F32),
-            vmem((2, n_view - 1, part, half), F32),
+            vmem((PIECES, n_view, part, width), F32),
+            vmem((PIECES, n_view - 1, part, width), F32),
             vmem((n_view, 8, 128), F32),
             vmem((n_view - 1, 8, 128), F32),
             vmem((n_img, part, feats), F32),
             dma((2,)), dma((chips,)),
-        ] + ring_sems + [dma((chips - 1, 2)), dma((chips - 1, 2)), dma((chips, 2)), dma((chips, 2))] + [
+        ] + ring_sems + [
+            dma((chips - 1, PIECES)), dma((chips - 1, PIECES)), dma((chips, PIECES)), dma((chips, PIECES))] + [
             dma((2, n_view - 1, 2)), dma((2, n_view - 1, 2)),
             dma((n_img - 1,)), dma((n_img - 1,)),
-            dma((2, n_view - 1)), dma((2, n_view - 1)),
+            dma((PIECES, n_view - 1)), dma((PIECES, n_view - 1)),
             dma((n_view - 1,)), dma((n_view - 1,)),
         ],
         compiler_params=pltpu.CompilerParams(

time: 76.1 us -> 74 us (0.972); the launches traced: 74.9 us -> 73.9 us
  Pallas kernels: 72.5 us -> 71.4 us
    pallas_call x1, Pallas kernels: 72.5 us -> 71.4 us  [on_device(): pl.pallas_call(functools.partial(kernel, n_img, n_view, beta), out_shape=...]
where the time goes in v4:
time: 74 us; the launch traced here: 73.9 us
  Pallas kernels  71.4 us (96%)
  local copies, waits for them, and re-layouts  2.45 us (3%)
    pallas_call x1, Pallas kernels, on_device(): pl.pallas_call(functools.partial(kernel, n_img, n_view, beta), out_shape=...  71.4 us
    unnamed x3, local copies, waits for them, and re-layouts  2.45 us

profile of v4, /device:TPU:1, one launch (start us, length us, event | category | flops | bytes accessed | tf_op | source)
XLA Modules:
  0.0 73.9 jit_solution(8157495033106555289)
XLA Ops:
  0.0 0.0 copy-start
  0.0 1.1 %copy-done = f32[2,96,1024]{2,1,0:T(8,128)S(1)} copy-done((f32[2,96,1024]{2,1,0:T(8,128)S(1)}, f32[2,96,1024]{2,1,0:T(8,128)}, u32[]{:S(2)}) %copy-start) | copy-done | bytes 786456
  1.1 71.4 %shard_map.28 = f32[8,64,1024]{2,1,0:T(8,128)S(1)} custom-call(f32[192,1024]{1,0:T(8,128)S(1)} %bitcast.3, f32[512,1024]{1,0:T(8,128)} %views_ref.1), custom_call_target="tpu_custom_call" | custom-call | flops 4831838208 | bytes 3145728 | tf_op jit(solution)/shard_map/pallas_call | solution.py:349
  72.5 1.3 %copy.4 = f32[512,1024]{1,0:T(8,128)} copy(f32[512,1024]{1,0:T(8,128)S(1)} %bitcast.2) | data formatting | bytes 4194304
Async XLA Ops:
  0.0 1.1 %copy-start = (f32[2,96,1024]{2,1,0:T(8,128)S(1)}, f32[2,96,1024]{2,1,0:T(8,128)}, u32[]{:S(2)}) copy-start(f32[2,96,1024]{2,1,0:T(8,128)} %param.2) | copy-start | bytes 2359300
